TPU v7x, 32 devices: a whole 2x2x4 slice. The times are simulated.
32 devices in a mesh: seq: 2 (over y), exp: 16 (over z, x, core).
Axes of the slice: x: 2, y: 2, z: 4, core: 2. Of those that a mesh axis runs over, the one named last changes fastest.
Arguments:
- tokens: bfloat16 [2048, 4096], P(('seq', 'exp')), may hold values from -6 to 6
- norm_gain: float32 [4096], replicated, may hold values from 0.1 to 1.9
- queries: bfloat16 [2048, 2048], P(('seq', 'exp')), may hold values from -24 to 24
- attn_keys: bfloat16 [2048, 2048], P(('seq', 'exp')), may hold values from -4.5 to 4.5
- attn_values: bfloat16 [2048, 2048], P(('seq', 'exp')), may hold values from -6 to 6
- expert_ids: int32 [2048, 2], P(('seq', 'exp')), may hold values from 0 to 63, all different within a row; in each aligned block of 64 rows (0 to 63, 64 to 127, ...) at most 2 rows name the same one
- route_weights: float32 [2048, 2], P(('seq', 'exp')), may hold values from 0.1 to 1
- gate_proj: bfloat16 [64, 1408, 4096], P('exp', 'seq'), may hold values from -0.09375 to 0.09375
- up_proj: bfloat16 [64, 1408, 4096], P('exp', 'seq'), may hold values from -0.09375 to 0.09375
- down_proj: bfloat16 [64, 1408, 4096], P('exp', 'seq'), may hold values from -0.15625 to 0.15625
Outputs:
- attention: bfloat16 [2048, 2048], P(('seq', 'exp'))
- expert_mix: bfloat16 [2048, 4096], P(('seq', 'exp'))
Inputs may be any that keep to these rules, and one draw needn't show every extreme that they name: `expert_ids`: the two experts of a token differ. Among the rows of one device (64 consecutive tokens, aligned), every expert is named exactly 2 times.
All inputs are finite; a program needn't handle non-finite values.
Results may differ from a plain program's by a relative error of at most 0.015.
Values may be sent and summed in bfloat16 or wider, within the bound.
No kernel may reach another device: no remote copies, remote signals or barrier semaphores. Data moves between devices by JAX's collectives and lax.ppermute only.
A program may use at most 128 MiB of HBM per device.

v0:
```python
import math

import jax
import jax.numpy as jnp
from jax import lax
from jax.sharding import PartitionSpec as P

EXPERTS = 64
HDIM = 64
SUMS = 64
SEG_DEV = 2
CAP = 2


EPS = 1e-05
NEG = -1e30


def broadcast(value, axis, source):
    kept = jnp.where(lax.axis_index(axis) == source, value, 0).astype(value.dtype)
    return lax.psum(kept, axis)


def normalize(tokens, norm_gain):
    values = tokens.astype(jnp.float32)
    inv_rms = lax.rsqrt(jnp.mean(values * values, axis=-1, keepdims=True) + EPS)
    return (values * inv_rms * norm_gain).astype(jnp.bfloat16)


def attend_block(
    query_blk, seg_keys, seg_values, sum_keys, sum_values, first_row, segment, score_scale
):
    local_sc = (
        jnp.einsum("qhd,khd->hqk", query_blk, seg_keys, preferred_element_type=jnp.float32)
        * score_scale
    )
    summ_sc = (
        jnp.einsum("qhd,khd->hqk", query_blk, sum_keys, preferred_element_type=jnp.float32)
        * score_scale
    )
    query_pos = first_row + jnp.arange(query_blk.shape[0], dtype=jnp.int32)
    key_pos = jnp.arange(seg_keys.shape[0], dtype=jnp.int32)
    local_ok = key_pos[None, :] <= query_pos[:, None]
    summ_ok = jnp.arange(sum_keys.shape[0], dtype=jnp.int32) // SUMS < segment
    local_sc = jnp.where(local_ok[None], local_sc, NEG)
    summ_sc = jnp.where(summ_ok[None, None], summ_sc, NEG)
    top_sc = jnp.maximum(
        jnp.max(local_sc, axis=-1, keepdims=True), jnp.max(summ_sc, axis=-1, keepdims=True)
    )
    local_ex = jnp.exp(local_sc - top_sc)
    summ_ex = jnp.exp(summ_sc - top_sc)
    totals = jnp.sum(local_ex, axis=-1, keepdims=True) + jnp.sum(summ_ex, axis=-1, keepdims=True)
    local_wt = (local_ex / totals).astype(jnp.bfloat16)
    summ_wt = (summ_ex / totals).astype(jnp.bfloat16)
    mixed_out = jnp.einsum("hqk,khd->qhd", local_wt, seg_values, preferred_element_type=jnp.float32)
    return mixed_out + jnp.einsum(
        "hqk,khd->qhd", summ_wt, sum_values, preferred_element_type=jnp.float32
    )


def slot_table(id_rows):
    onehot = (id_rows[..., None] == jnp.arange(EXPERTS, dtype=jnp.int32)).astype(jnp.int32)
    before = jnp.cumsum(onehot, axis=-2) - onehot
    return jnp.sum(before * onehot, axis=-1)


def fill_slots(rows, slot_pos, slot_total):
    row_count = rows.shape[0]
    padded = jnp.concatenate([rows, jnp.zeros((1, rows.shape[1]), rows.dtype)], axis=0)
    source_row = jnp.arange(row_count * 2, dtype=jnp.int32) // 2
    index_table = jnp.full((slot_total,), row_count, jnp.int32).at[slot_pos].set(source_row)
    return padded[index_table]


def expert_block(row_block, gate_proj, up_proj, down_proj):
    gate_act = jnp.einsum(
        "...ecd,efd->...ecf", row_block, gate_proj, preferred_element_type=jnp.float32
    )
    up_act = jnp.einsum(
        "...ecd,efd->...ecf", row_block, up_proj, preferred_element_type=jnp.float32
    )
    hidden = (jax.nn.silu(gate_act) * up_act).astype(jnp.bfloat16)
    return jnp.einsum("...ecf,efd->...ecd", hidden, down_proj, preferred_element_type=jnp.float32)


def on_device(
    tokens,
    norm_gain,
    queries,
    attn_keys,
    attn_values,
    expert_ids,
    route_weights,
    gate_proj,
    up_proj,
    down_proj,
):
    exp_count = lax.axis_size("exp")
    seq_count = lax.axis_size("seq")
    local_tokens = tokens.shape[0]
    feature_count = tokens.shape[1]
    normed = normalize(tokens, norm_gain)
    head_q, head_k, head_v = (
        lax.all_to_all(queries, "exp", split_axis=1, concat_axis=0, tiled=True),
        lax.all_to_all(attn_keys, "exp", split_axis=1, concat_axis=0, tiled=True),
        lax.all_to_all(attn_values, "exp", split_axis=1, concat_axis=0, tiled=True),
    )
    heads_dev = head_q.shape[1] // HDIM
    seg_len = head_q.shape[0] // SEG_DEV
    block_len = seg_len // SUMS
    head_q = head_q.reshape(SEG_DEV, seg_len, heads_dev, HDIM)
    head_k = head_k.reshape(SEG_DEV, seg_len, heads_dev, HDIM)
    head_v = head_v.reshape(SEG_DEV, seg_len, heads_dev, HDIM)
    inv_block = 1.0 / math.sqrt(block_len)
    sum_k = (
        jnp.sum(
            head_k.astype(jnp.float32).reshape(SEG_DEV, SUMS, block_len, heads_dev, HDIM), axis=2
        )
        * inv_block
    ).astype(jnp.bfloat16)
    sum_v = (
        jnp.sum(
            head_v.astype(jnp.float32).reshape(SEG_DEV, SUMS, block_len, heads_dev, HDIM), axis=2
        )
        * inv_block
    ).astype(jnp.bfloat16)
    sum_k = sum_k.reshape(SEG_DEV * SUMS, heads_dev, HDIM)
    sum_v = sum_v.reshape(SEG_DEV * SUMS, heads_dev, HDIM)
    key_list = []
    value_list = []
    for root_index in range(seq_count):
        recv_keys, recv_values = (
            broadcast(sum_k, "seq", root_index),
            broadcast(sum_v, "seq", root_index),
        )
        key_list.append(recv_keys)
        value_list.append(recv_values)
    all_keys = jnp.concatenate(key_list, axis=0)
    all_values = jnp.concatenate(value_list, axis=0)
    query_rows = min(512, seg_len)
    score_scale = 1.0 / math.sqrt(HDIM)
    seg_base = lax.axis_index("seq") * SEG_DEV
    pieces = []
    for local_seg in range(SEG_DEV):
        for first_row in range(0, seg_len, query_rows):
            block_out = attend_block(
                head_q[local_seg, first_row : first_row + query_rows],
                head_k[local_seg],
                head_v[local_seg],
                all_keys,
                all_values,
                first_row,
                seg_base + local_seg,
                score_scale,
            )
            pieces.append(block_out.astype(jnp.bfloat16))
    head_out = jnp.concatenate(pieces, axis=0).reshape(SEG_DEV * seg_len, heads_dev * HDIM)
    attention = lax.all_to_all(head_out, "exp", split_axis=0, concat_axis=1, tiled=True)
    exp_dev = EXPERTS // exp_count
    flat_ids = expert_ids.reshape(-1)
    local_pos = flat_ids * CAP + slot_table(flat_ids)
    send_rows = fill_slots(normed, local_pos, EXPERTS * CAP)
    send_rows = send_rows.reshape(exp_count, exp_dev * CAP, feature_count)
    recv_rows = lax.all_to_all(send_rows, "exp", split_axis=0, concat_axis=0, tiled=True)
    gathered = lax.all_gather(recv_rows, "seq", axis=0, tiled=True).reshape(
        seq_count * exp_count, exp_dev, CAP, feature_count
    )
    summed = lax.psum_scatter(
        expert_block(gathered, gate_proj, up_proj, down_proj).astype(jnp.bfloat16),
        "seq",
        scatter_dimension=0,
        tiled=True,
    )
    owner_out = summed.reshape(exp_count, exp_dev * CAP, feature_count)
    source_out = lax.all_to_all(owner_out, "exp", split_axis=0, concat_axis=0, tiled=True).reshape(
        EXPERTS * CAP, feature_count
    )
    picked = source_out[local_pos].astype(jnp.float32).reshape(local_tokens, 2, feature_count)
    expert_mix = jnp.sum(route_weights[:, :, None] * picked, axis=1).astype(jnp.bfloat16)
    return (attention, expert_mix)


def solution(mesh):
    return jax.shard_map(
        on_device,
        mesh=mesh,
        in_specs=(
            P(("seq", "exp"), None),
            P(),
            P(("seq", "exp"), None),
            P(("seq", "exp"), None),
            P(("seq", "exp"), None),
            P(("seq", "exp"), None),
            P(("seq", "exp"), None),
            P("exp", "seq", None),
            P("exp", "seq", None),
            P("exp", "seq", None),
        ),
        out_specs=(P(("seq", "exp"), None), P(("seq", "exp"), None)),
        check_vma=False,
    )
```

profile of v0, /device:TPU:0, one launch (start us, length us, event | category | flops | bytes accessed | tf_op | source)
XLA Modules:
  0.0 205.4 jit_solution(13110247816437100272)
XLA Ops:
  10.5 1.2 fusion.36
  11.8 1.2 fusion.38
  13.1 2.2 %gather_fusion = bf16[128,4096]{1,0:T(8,128)(2,1)} fusion(bf16[65,4096]{1,0:T(8,128)(2,1)S(1)} %concatenate.15, s32[1024]{0:T(1024)S(1)} %pad_clamp_fusion.1), kind=kCustom, calls=%fused_computation | custom fusion | bytes 2097664 | tf_op jit(solution)/shard_map/gather | solution.py:72
  15.3 7.5 %all-to-all-start.4 = ((bf16[16,8,4096]{2,1,0:T(8,128)(2,1)}), bf16[16,8,4096]{2,1,0:T(8,128)(2,1)S(1)}, u32[]{:S(2)}, u32[]{:S(2)}) async-start(bf16[16,8,4096]{2,1,0:T(8,128)(2,1)} %bitcast.16), calls=%async_computation.4 | async-start | bytes 2097152 | tf_op jit(solution)/shard_map/all_to_all | solution.py:164
  23.6 22.1 %all-to-all-done.4 = bf16[16,8,4096]{2,1,0:T(8,128)(2,1)S(1)} async-done(((bf16[16,8,4096]{2,1,0:T(8,128)(2,1)}), bf16[16,8,4096]{2,1,0:T(8,128)(2,1)S(1)}, u32[]{:S(2)}, u32[]{:S(2)}) %all-to-all-start.4) | async-done | bytes 1048608 | tf_op jit(solution)/shard_map/all_to_all | solution.py:164
  45.7 6.9 %all-to-all-start.1 = ((bf16[64,16,128]{2,0,1:T(8,128)(2,1)}), bf16[64,16,128]{2,0,1:T(8,128)(2,1)S(1)}, u32[]{:S(2)}, u32[]{:S(2)}) async-start(bf16[64,16,128]{2,0,1:T(8,128)(2,1)} %copy_bitcast_fusion.2), calls=%async_computation.1 | async-start | bytes 524288 | tf_op jit(solution)/shard_map/all_to_all | solution.py:105
  54.1 8.5 %all-to-all-done.1 = bf16[64,16,128]{2,0,1:T(8,128)(2,1)S(1)} async-done(((bf16[64,16,128]{2,0,1:T(8,128)(2,1)}), bf16[64,16,128]{2,0,1:T(8,128)(2,1)S(1)}, u32[]{:S(2)}, u32[]{:S(2)}) %all-to-all-start.1) | async-done | bytes 262176 | tf_op jit(solution)/shard_map/all_to_all | solution.py:105
  62.6 3.5 %all-to-all-start.2 = ((bf16[64,16,128]{2,0,1:T(8,128)(2,1)}), bf16[64,16,128]{2,0,1:T(8,128)(2,1)S(1)}, u32[]{:S(2)}, u32[]{:S(2)}) async-start(bf16[64,16,128]{2,0,1:T(8,128)(2,1)} %copy_bitcast_fusion.3), calls=%async_computation.2 | async-start | bytes 524288 | tf_op jit(solution)/shard_map/all_to_all | solution.py:106
  67.1 9.1 %all-to-all-done.2 = bf16[64,16,128]{2,0,1:T(8,128)(2,1)S(1)} async-done(((bf16[64,16,128]{2,0,1:T(8,128)(2,1)}), bf16[64,16,128]{2,0,1:T(8,128)(2,1)S(1)}, u32[]{:S(2)}, u32[]{:S(2)}) %all-to-all-start.2) | async-done | bytes 262176 | tf_op jit(solution)/shard_map/all_to_all | solution.py:106
  76.2 4.2 %all-to-all-start = ((bf16[64,16,128]{2,0,1:T(8,128)(2,1)}), bf16[64,16,128]{2,0,1:T(8,128)(2,1)}, u32[]{:S(2)}, u32[]{:S(2)}) async-start(bf16[64,16,128]{2,0,1:T(8,128)(2,1)} %copy_bitcast_fusion.1), calls=%async_computation | async-start | bytes 524288 | tf_op jit(solution)/shard_map/all_to_all | solution.py:104
  86.8 3.7 %all-to-all-done = bf16[64,16,128]{2,0,1:T(8,128)(2,1)} async-done(((bf16[64,16,128]{2,0,1:T(8,128)(2,1)}), bf16[64,16,128]{2,0,1:T(8,128)(2,1)}, u32[]{:S(2)}, u32[]{:S(2)}) %all-to-all-start) | async-done | bytes 262176 | tf_op jit(solution)/shard_map/all_to_all | solution.py:104
  91.7 2.7 %copy.121 = bf16[32,8,4096]{2,0,1:T(8,128)(2,1)S(1)} copy(bf16[32,8,4096]{2,1,0:T(8,128)(2,1)} %all-gather.2.cloned.1.call-done) | data formatting | bytes 4194304 | tf_op jit(solution)/shard_map/all_gather | solution.py:165
  94.5 11.3 %fusion.20 = f32[32,4,2,704]{3,0,2,1:T(8,128)S(1)} fusion(bf16[32,4,2,4096]{3,0,2,1:T(8,128)(2,1)S(1)} %bitcast.111, bf16[4,704,4096]{2,1,0:T(8,128)(2,1)} %param.17), kind=kOutput, calls=%fused_computation.30 | convolution fusion | flops 1476395008 | bytes 25886720 | tf_op jit(solution)/shard_map/...ecd,efd->...ecf/dot_general | solution.py:76
  105.8 11.8 %fusion.29 = bf16[32,4,2,704]{3,0,2,1:T(8,128)(2,1)S(1)} fusion(bf16[32,4,2,4096]{3,0,2,1:T(8,128)(2,1)S(1)} %bitcast.112, bf16[4,704,4096]{2,1,0:T(8,128)(2,1)} %param.18, f32[32,4,2,704]{3,0,2,1:T(8,128)S(1)} %fusion.20), kind=kOutput, calls=%fused_computation.33 | convolution fusion | flops 1477476352 | bytes 26247168 | tf_op jit(solution)/shard_map/...ecd,efd->...ecf/dot_general | solution.py:79
  117.6 13.2 %fusion.9 = bf16[32,4,2,4096]{3,0,2,1:T(8,128)(2,1)} fusion(bf16[32,4,2,704]{3,0,2,1:T(8,128)(2,1)S(1)} %fusion.29, bf16[4,704,4096]{2,1,0:T(8,128)(2,1)} %param.19), kind=kOutput, calls=%fused_computation.10 | convolution fusion | flops 1477443584 | bytes 25526272 | tf_op jit(solution)/shard_map/...ecf,efd->...ecd/dot_general | solution.py:83
  132.1 1.8 fusion.12
  142.1 3.5 %all-to-all-start.3 = ((bf16[16,64,128]{2,1,0:T(8,128)(2,1)}), bf16[16,64,128]{2,1,0:T(8,128)(2,1)S(1)}, u32[]{:S(2)}, u32[]{:S(2)}) async-start(bf16[16,64,128]{2,1,0:T(8,128)(2,1)} %copy.116), calls=%async_computation.3 | async-start | bytes 524288 | tf_op jit(solution)/shard_map/all_to_all | solution.py:158
  145.6 15.4 %reduce-scatter.2.cloned.1.call-done = bf16[16,4,2,4096]{3,0,2,1:T(8,128)(2,1)} async-done(((bf16[32,4,2,4096]{3,0,2,1:T(8,128)(2,1)}), bf16[16,4,2,4096]{3,0,2,1:T(8,128)(2,1)}) %reduce-scatter.2.cloned.1.call-update) | async-done | bytes 1048592 | tf_op jit(solution)/shard_map/reduce_scatter | solution.py:168
  161.1 2.8 %copy.122 = bf16[16,8,4096]{2,1,0:T(8,128)(2,1)} copy(bf16[16,8,4096]{2,0,1:T(8,128)(2,1)} %bitcast.115) | data formatting | bytes 2097152 | tf_op jit(solution)/shard_map/reshape | solution.py:174
  163.9 5.6 %all-to-all-start.5 = ((bf16[16,8,4096]{2,1,0:T(8,128)(2,1)}), bf16[16,8,4096]{2,1,0:T(8,128)(2,1)S(1)}, u32[]{:S(2)}, u32[]{:S(2)}) async-start(bf16[16,8,4096]{2,1,0:T(8,128)(2,1)} %copy.122), calls=%async_computation.6 | async-start | bytes 2097152 | tf_op jit(solution)/shard_map/all_to_all | solution.py:175
  170.4 22.1 %all-to-all-done.5 = bf16[16,8,4096]{2,1,0:T(8,128)(2,1)S(1)} async-done(((bf16[16,8,4096]{2,1,0:T(8,128)(2,1)}), bf16[16,8,4096]{2,1,0:T(8,128)(2,1)S(1)}, u32[]{:S(2)}, u32[]{:S(2)}) %all-to-all-start.5) | async-done | bytes 1048608 | tf_op jit(solution)/shard_map/all_to_all | solution.py:175
  192.4 1.2 gather_fusion.1
  193.7 1.3 reshape.181
  195.0 3.9 %multiply_reduce_fusion = bf16[64,4096]{1,0:T(8,128)(2,1)} fusion(f32[64,2,4096]{2,1,0:T(2,128)S(1)} %reshape.181, f32[64,2]{1,0:T(8,128)S(1)} %copy.118), kind=kLoop, calls=%fused_computation.11 | loop fusion | flops 786432 | bytes 2621952 | tf_op jit(solution)/shard_map/reduce_sum | solution.py:179
  (94 shorter events, 24.2 us)
Async XLA Ops:
  7.2 15.6 %copy-start = (bf16[64,2048]{1,0:T(8,128)(2,1)S(1)}, bf16[64,2048]{1,0:T(8,128)(2,1)}, u32[]{:S(2)}) copy-start(bf16[64,2048]{1,0:T(8,128)(2,1)} %param.13) | copy-start | bytes 786436
  15.3 38.1 %copy-start.3 = (bf16[64,2048]{1,0:T(8,128)(2,1)S(1)}, bf16[64,2048]{1,0:T(8,128)(2,1)}, u32[]{:S(2)}) copy-start(bf16[64,2048]{1,0:T(8,128)(2,1)} %param.14) | copy-start | bytes 786436
  15.3 30.4 %all-to-all-start.4 = ((bf16[16,8,4096]{2,1,0:T(8,128)(2,1)}), bf16[16,8,4096]{2,1,0:T(8,128)(2,1)S(1)}, u32[]{:S(2)}, u32[]{:S(2)}) async-start(bf16[16,8,4096]{2,1,0:T(8,128)(2,1)} %bitcast.16), calls=%async_computation.4 | async-start | bytes 2097152 | tf_op jit(solution)/shard_map/all_to_all | solution.py:164
  22.8 43.5 %copy-start.4 = (bf16[64,2048]{1,0:T(8,128)(2,1)S(1)}, bf16[64,2048]{1,0:T(8,128)(2,1)}, u32[]{:S(2)}) copy-start(bf16[64,2048]{1,0:T(8,128)(2,1)} %param.12) | copy-start | bytes 786436
  45.7 6.9 %copy-start.2 = (bf16[16,8,4096]{2,1,0:T(8,128)(2,1)}, bf16[16,8,4096]{2,1,0:T(8,128)(2,1)S(1)}, u32[]{:S(2)}) copy-start(bf16[16,8,4096]{2,1,0:T(8,128)(2,1)S(1)} %all-to-all-done.4) | copy-start | bytes 3145732
  45.7 16.9 %all-to-all-start.1 = ((bf16[64,16,128]{2,0,1:T(8,128)(2,1)}), bf16[64,16,128]{2,0,1:T(8,128)(2,1)S(1)}, u32[]{:S(2)}, u32[]{:S(2)}) async-start(bf16[64,16,128]{2,0,1:T(8,128)(2,1)} %copy_bitcast_fusion.2), calls=%async_computation.1 | async-start | bytes 524288 | tf_op jit(solution)/shard_map/all_to_all | solution.py:105
  52.6 39.1 %all-gather.2.cloned.1.call-start = ((), (), s32[]{:S(2)}) async-start(), calls=%async_computation.7 | async-start | bytes 3145728 | tf_op jit(solution)/shard_map/all_gather | solution.py:165
  62.6 13.6 %all-to-all-start.2 = ((bf16[64,16,128]{2,0,1:T(8,128)(2,1)}), bf16[64,16,128]{2,0,1:T(8,128)(2,1)S(1)}, u32[]{:S(2)}, u32[]{:S(2)}) async-start(bf16[64,16,128]{2,0,1:T(8,128)(2,1)} %copy_bitcast_fusion.3), calls=%async_computation.2 | async-start | bytes 524288 | tf_op jit(solution)/shard_map/all_to_all | solution.py:106
  76.2 14.2 %all-to-all-start = ((bf16[64,16,128]{2,0,1:T(8,128)(2,1)}), bf16[64,16,128]{2,0,1:T(8,128)(2,1)}, u32[]{:S(2)}, u32[]{:S(2)}) async-start(bf16[64,16,128]{2,0,1:T(8,128)(2,1)} %copy_bitcast_fusion.1), calls=%async_computation | async-start | bytes 524288 | tf_op jit(solution)/shard_map/all_to_all | solution.py:104
  80.4 53.5 %all-reduce.4.cloned.1.call-start = ((), (), s32[]{:S(2)}) async-start(), calls=%async_computation.9 | async-start | bytes 262144 | tf_op jit(solution)/shard_map/psum | solution.py:21
  91.5 69.6 %reduce-scatter.2.cloned.1.call-start = ((), (), s32[]{:S(2)}) async-start(), calls=%async_computation.8 | async-start | bytes 3145728 | tf_op jit(solution)/shard_map/reduce_scatter | solution.py:168
  133.9 2.3 %copy-start.8 = (f32[2,512,512]{1,2,0:T(8,128)S(1)}, f32[2,512,512]{1,2,0:T(8,128)}, u32[]{:S(2)}) copy-start(f32[2,512,512]{1,2,0:T(8,128)} %get-tuple-element.19) | copy-start | bytes 6291460
  137.2 1.1 copy-start.6
  137.2 1.1 copy-start.5
  142.1 21.8 %all-to-all-start.3 = ((bf16[16,64,128]{2,1,0:T(8,128)(2,1)}), bf16[16,64,128]{2,1,0:T(8,128)(2,1)S(1)}, u32[]{:S(2)}, u32[]{:S(2)}) async-start(bf16[16,64,128]{2,1,0:T(8,128)(2,1)} %copy.116), calls=%async_computation.3 | async-start | bytes 524288 | tf_op jit(solution)/shard_map/all_to_all | solution.py:158
  161.1 8.5 %copy-start.7 = (f32[64,2]{0,1:T(2,128)S(1)}, f32[64,2]{0,1:T(2,128)}, u32[]{:S(2)}) copy-start(f32[64,2]{0,1:T(2,128)} %param.16) | copy-start | bytes 1540
  163.9 28.6 %all-to-all-start.5 = ((bf16[16,8,4096]{2,1,0:T(8,128)(2,1)}), bf16[16,8,4096]{2,1,0:T(8,128)(2,1)S(1)}, u32[]{:S(2)}, u32[]{:S(2)}) async-start(bf16[16,8,4096]{2,1,0:T(8,128)(2,1)} %copy.122), calls=%async_computation.6 | async-start | bytes 2097152 | tf_op jit(solution)/shard_map/all_to_all | solution.py:175
  193.6 5.3 %copy-start.1 = (bf16[64,2048]{1,0:T(8,128)(2,1)S(1)}, bf16[64,2048]{1,0:T(8,128)(2,1)}, u32[]{:S(2)}) copy-start(bf16[64,2048]{1,0:T(8,128)(2,1)} %param.13) | copy-start | bytes 786436
Sparse Core Ops, SparseCore 0:
  55.0 34.4 all-gather.1
  92.5 21.8 all-reduce.3
  131.0 30.0 reduce-scatter.1
where the time goes:
time: 207 us; the launch traced here: 205 us
  waiting for transfers between devices  81.7 us (39%)
  matrix products  42.1 us (20%)
  starting transfers between devices  31.6 us (15%)
  local copies, waits for them, and re-layouts  25.1 us (12%)
  between operations  14.3 us (7%)
  other arithmetic  10.8 us (5%)
    all_to_all x1, waiting for transfers between devices, on_device(): lax.all_to_all(send_rows, 'exp', split_axis=0, concat_axis=0, tiled=True)  22.1 us
    all_to_all x1, waiting for transfers between devices, on_device(): lax.all_to_all(owner_out, 'exp', split_axis=0, concat_axis=0, tiled=True)  22.1 us
    reduce_scatter x1, waiting for transfers between devices, on_device(): lax.psum_scatter(expert_block(gathered, gate_proj, up_proj, down_proj).as...  15.4 us
    dot_general x1, matrix products, expert_block(): jnp.einsum('...ecf,efd->...ecd', hidden, down_proj, preferred_element_typ...  13.2 us
    dot_general x1, matrix products, expert_block(): jnp.einsum('...ecd,efd->...ecf', row_block, up_proj, preferred_element_ty...  11.8 us
    dot_general x1, matrix products, expert_block(): jnp.einsum('...ecd,efd->...ecf', row_block, gate_proj, preferred_element_...  11.3 us
    all_to_all x1, waiting for transfers between devices, on_device(): lax.all_to_all(attn_values, 'exp', split_axis=1, concat_axis=0, tiled=True)  9.1 us
    all_to_all x1, waiting for transfers between devices, on_device(): lax.all_to_all(attn_keys, 'exp', split_axis=1, concat_axis=0, tiled=True)  8.52 us
  transfers between devices with their start and end apart: 9, of which 6 were waited for; matrix products, arithmetic and copies ran while one was open for 31% of the time, Pallas kernels for 0%

commit v1 on v0

v1 whole, which is shorter than its diff:
```python
import functools
import math

import jax
import jax.numpy as jnp
from jax import lax
from jax.experimental import pallas as pl
from jax.experimental.pallas import tpu as pltpu
from jax.sharding import PartitionSpec as P

EXPERTS = 64
HDIM = 64
SUMS = 64
SEG_DEV = 2
CAP = 2
CHUNKS = 2

EPS = 1e-05
NEG = -1e30
F32 = jnp.float32
BF16 = jnp.bfloat16

VMEM = pl.BlockSpec(memory_space=pltpu.VMEM)
ANY = pl.BlockSpec(memory_space=pl.ANY)
SMEM = pl.BlockSpec(memory_space=pltpu.SMEM)


def params(mib):
    return pltpu.CompilerParams(vmem_limit_bytes=mib * 2**20)


def as_row(column):
    n = column.shape[0]
    eye = lax.broadcasted_iota(jnp.int32, (n, n), 0) == lax.broadcasted_iota(jnp.int32, (n, n), 1)
    return jnp.sum(jnp.where(eye, column, 0), axis=0, keepdims=True)


def slots(ids):
    n = ids.shape[0]
    columns = [ids[:, 0:1], ids[:, 1:2]]
    rows = [as_row(column) for column in columns]
    earlier = lax.broadcasted_iota(jnp.int32, (n, n), 1) < lax.broadcasted_iota(jnp.int32, (n, n), 0)
    found = []
    for column in columns:
        same = (rows[0] == column) | (rows[1] == column)
        before = jnp.sum(jnp.where(same & earlier, 1, 0), axis=1, keepdims=True)
        found.append(column * CAP + before)
    return found


def prep_kernel(tok_ref, gain_ref, ids_ref, *out_refs):
    n = tok_ref.shape[0]
    values = tok_ref[...].astype(F32)
    inv_rms = lax.rsqrt(jnp.mean(values * values, axis=-1, keepdims=True) + EPS)
    normed = (values * inv_rms * gain_ref[...]).astype(BF16)
    first, second = [as_row(column) for column in slots(ids_ref[...])]
    place = lax.broadcasted_iota(jnp.int32, (EXPERTS * CAP, n), 0)
    pick = jnp.where((place == first) | (place == second), 1.0, 0.0).astype(BF16)
    rows = jnp.dot(pick, normed, preferred_element_type=F32)
    dests, step = out_refs[0].shape[0], out_refs[0].shape[1]
    for dest in range(dests):
        for chunk, out_ref in enumerate(out_refs):
            lower = (dest * len(out_refs) + chunk) * step
            out_ref[dest] = rows[lower : lower + step].astype(BF16)


def pack_kernel(q_ref, k_ref, v_ref, out_ref):
    width = out_ref.shape[3]
    for dest in range(out_ref.shape[0]):
        for which, ref in enumerate((q_ref, k_ref, v_ref)):
            out_ref[dest, which] = ref[:, dest * width : (dest + 1) * width]


def sums_kernel(block, recv_ref, out_ref):
    sources, _, tokens, width = recv_ref.shape
    per_source = tokens // block
    total = sources * tokens
    row = lax.broadcasted_iota(jnp.int32, (total // block, total), 0)
    column = lax.broadcasted_iota(jnp.int32, (total // block, total), 1)
    member = jnp.where(column // block == row, 1.0, 0.0).astype(BF16)
    for which in (1, 2):
        values = recv_ref[:, which].reshape(total, width)
        summed = jnp.dot(member, values, preferred_element_type=F32) * (1.0 / math.sqrt(block))
        out_ref[which - 1] = summed.astype(BF16)


def attend_kernel(query_rows, seg_ref, recv_ref, *refs):
    sum_refs, out_ref = refs[:-1], refs[-1]
    sources, _, tokens, width = recv_ref.shape
    seg_len = sources * tokens
    query, key, value = (recv_ref[:, which].reshape(seg_len, width) for which in range(3))
    sum_keys = jnp.concatenate([ref[0] for ref in sum_refs], axis=0)
    sum_values = jnp.concatenate([ref[1] for ref in sum_refs], axis=0)
    sum_total = sum_keys.shape[0]
    scale = 1.0 / math.sqrt(HDIM)
    seen = seg_ref[0] * SUMS
    lane = lax.broadcasted_iota(jnp.int32, (1, width), 1)
    nt = (((1,), (1,)), ((), ()))
    for first in range(0, seg_len, query_rows):
        last = first + query_rows
        local_ok = (
            lax.broadcasted_iota(jnp.int32, (query_rows, last), 1)
            <= lax.broadcasted_iota(jnp.int32, (query_rows, last), 0) + first
        )
        summ_ok = lax.broadcasted_iota(jnp.int32, (query_rows, sum_total), 1) < seen
        mixed = jnp.zeros((query_rows, width), F32)
        for head in range(width // HDIM):
            mine = (lane >= head * HDIM) & (lane < (head + 1) * HDIM)
            rows = jnp.where(mine, query[first:last], jnp.zeros((), BF16))
            local_sc = lax.dot_general(rows, key[:last], nt, preferred_element_type=F32) * scale
            summ_sc = lax.dot_general(rows, sum_keys, nt, preferred_element_type=F32) * scale
            local_sc = jnp.where(local_ok, local_sc, NEG)
            summ_sc = jnp.where(summ_ok, summ_sc, NEG)
            top = jnp.maximum(
                jnp.max(local_sc, axis=-1, keepdims=True), jnp.max(summ_sc, axis=-1, keepdims=True)
            )
            local_ex = jnp.exp(local_sc - top)
            summ_ex = jnp.exp(summ_sc - top)
            inv = 1.0 / (
                jnp.sum(local_ex, axis=-1, keepdims=True) + jnp.sum(summ_ex, axis=-1, keepdims=True)
            )
            got = jnp.dot((local_ex * inv).astype(BF16), value[:last], preferred_element_type=F32)
            got += jnp.dot((summ_ex * inv).astype(BF16), sum_values, preferred_element_type=F32)
            mixed = jnp.where(mine, got, mixed)
        out_ref[first:last] = mixed.astype(BF16)


def ffn_kernel(base, planes, *refs):
    row_refs, (gate_ref, up_ref, down_ref) = refs[:planes], refs[planes : planes + 3]
    out_refs = refs[planes + 3 : 2 * planes + 3]
    buf, x_ref, y_ref, sem = refs[2 * planes + 3 :]
    sources, step, width = row_refs[0].shape
    experts = step // CAP
    copies = []
    for expert in range(experts):
        for which, ref in enumerate((gate_ref, up_ref, down_ref)):
            at = expert * 3 + which
            copy = pltpu.make_async_copy(ref.at[base + expert], buf.at[at], sem.at[at])
            copy.start()
            copies.append(copy)
    total = planes * sources * step
    for plane in range(planes):
        for source in range(sources):
            lower = (plane * sources + source) * step
            y_ref[lower : lower + step] = row_refs[plane][source].astype(F32)
    to = lax.broadcasted_iota(jnp.int32, (total, total), 0)
    frm = lax.broadcasted_iota(jnp.int32, (total, total), 1)
    per = total // experts
    order = (to % per // CAP) * step + (to // per) * CAP + to % CAP
    sort = jnp.where(frm == order, 1.0, 0.0).astype(BF16)
    x_ref[...] = jnp.dot(sort, y_ref[...].astype(BF16), preferred_element_type=F32).astype(BF16)
    nt = (((1,), (1,)), ((), ()))
    for expert in range(experts):
        rows = x_ref[expert * per : (expert + 1) * per]
        copies[expert * 3].wait()
        gate = lax.dot_general(rows, buf[expert * 3], nt, preferred_element_type=F32)
        copies[expert * 3 + 1].wait()
        up = lax.dot_general(rows, buf[expert * 3 + 1], nt, preferred_element_type=F32)
        hidden = (gate / (1.0 + jnp.exp(-gate)) * up).astype(BF16)
        copies[expert * 3 + 2].wait()
        piece = jnp.dot(hidden, buf[expert * 3 + 2], preferred_element_type=F32)
        x_ref[expert * per : (expert + 1) * per] = piece.astype(BF16)
    inverse = (to // step) * CAP + (to % step // CAP) * per + to % CAP
    unsort = jnp.where(frm == inverse, 1.0, 0.0).astype(BF16)
    y_ref[...] = jnp.dot(unsort, x_ref[...], preferred_element_type=F32)
    for plane in range(planes):
        for source in range(sources):
            lower = (plane * sources + source) * step
            out_refs[plane][source] = y_ref[lower : lower + step].astype(BF16)


def mix_kernel(ids_ref, weight_ref, *refs):
    in_refs, out_ref, y_ref = refs[:-2], refs[-2], refs[-1]
    dests, step = in_refs[0].shape[0], in_refs[0].shape[1]
    for dest in range(dests):
        for chunk, ref in enumerate(in_refs):
            lower = (dest * len(in_refs) + chunk) * step
            y_ref[lower : lower + step] = ref[dest].astype(F32)
    rows = y_ref[...].astype(BF16)
    n = ids_ref.shape[0]
    place = lax.broadcasted_iota(jnp.int32, (n, EXPERTS * CAP), 1)
    total = None
    for k, column in enumerate(slots(ids_ref[...])):
        pick = jnp.where(place == column, 1.0, 0.0).astype(BF16)
        part = weight_ref[:, k : k + 1] * jnp.dot(pick, rows, preferred_element_type=F32)
        total = part if total is None else total + part
    out_ref[...] = total.astype(BF16)


def shape(dims, kind=BF16):
    return jax.ShapeDtypeStruct(dims, kind)


def on_device(
    tokens,
    norm_gain,
    queries,
    attn_keys,
    attn_values,
    expert_ids,
    route_weights,
    gate_proj,
    up_proj,
    down_proj,
):
    exp_count = lax.axis_size("exp")
    seq_count = lax.axis_size("seq")
    local_tokens, features = tokens.shape
    exp_dev, hidden = gate_proj.shape[0], gate_proj.shape[1]
    chunks = CHUNKS
    experts = exp_dev // chunks
    step = experts * CAP
    group = exp_count // SEG_DEV
    seg_len = group * local_tokens
    segs = seq_count * SEG_DEV
    att = queries.shape[1]
    width = att // group
    everyone = ("seq", "exp")

    send = pl.pallas_call(
        prep_kernel,
        out_shape=[shape((exp_count, step, features))] * chunks,
        in_specs=[VMEM] * 3,
        out_specs=[VMEM] * chunks,
        compiler_params=params(32),
        name="prep",
    )(tokens, norm_gain.reshape(1, -1), expert_ids)

    packed = pl.pallas_call(
        pack_kernel,
        out_shape=shape((group, 3, local_tokens, width)),
        in_specs=[VMEM] * 3,
        out_specs=VMEM,
        compiler_params=params(32),
        name="pack",
    )(queries, attn_keys, attn_values)
    halves = [[half * group + j for j in range(group)] for half in range(SEG_DEV)]
    got = lax.all_to_all(packed, "exp", 0, 0, axis_index_groups=halves, tiled=True)

    recv = [lax.all_to_all(rows, "exp", 0, 0, tiled=True) for rows in send]

    sums = pl.pallas_call(
        functools.partial(sums_kernel, seg_len // SUMS),
        out_shape=shape((2, SUMS, width)),
        in_specs=[VMEM],
        out_specs=VMEM,
        compiler_params=params(32),
        name="sums",
    )(got)

    def device(segment, j):
        return (segment // SEG_DEV) * exp_count + (segment % SEG_DEV) * group + j

    segment = lax.axis_index("seq") * SEG_DEV + lax.axis_index("exp") // group
    parts = []
    for back in range(1, segs):
        pairs = [
            (device(frm, j), device(frm + back, j)) for frm in range(segs - back) for j in range(group)
        ]
        parts.append(lax.ppermute(sums, everyone, pairs))
    head_out = pl.pallas_call(
        functools.partial(attend_kernel, min(256, seg_len)),
        out_shape=shape((seg_len, width)),
        in_specs=[SMEM, VMEM] + [VMEM] * (segs - 1),
        out_specs=VMEM,
        compiler_params=params(48),
        name="attend",
    )(segment.reshape(1).astype(jnp.int32), got, *parts)
    attention = lax.all_to_all(
        head_out.reshape(group, local_tokens, width), "exp", 0, 0, axis_index_groups=halves, tiled=True
    )
    attention = attention.transpose(1, 0, 2).reshape(local_tokens, att)

    mine = []
    for chunk in range(chunks):
        planes = [recv[chunk]]
        for other in range(1, seq_count):
            pairs = [(i, i ^ other) for i in range(seq_count)]
            planes.append(lax.ppermute(recv[chunk], "seq", pairs))
        total = seq_count * exp_count * step
        pieces = pl.pallas_call(
            functools.partial(ffn_kernel, chunk * experts, seq_count),
            out_shape=[shape((exp_count, step, features))] * seq_count,
            in_specs=[VMEM] * seq_count + [ANY] * 3,
            out_specs=[VMEM] * seq_count,
            scratch_shapes=[
                pltpu.VMEM((experts * 3, hidden, features), BF16),
                pltpu.VMEM((total, features), BF16),
                pltpu.VMEM((total, features), F32),
                pltpu.SemaphoreType.DMA((experts * 3,)),
            ],
            compiler_params=params(56),
            cost_estimate=pl.CostEstimate(
                flops=6 * total * hidden * features,
                bytes_accessed=experts * 3 * hidden * features * 2,
                transcendentals=total * hidden,
            ),
            name="experts",
        )(*planes, gate_proj, up_proj, down_proj)
        summed = pieces[0].astype(F32)
        for other in range(1, seq_count):
            pairs = [(i, i ^ other) for i in range(seq_count)]
            summed = summed + lax.ppermute(pieces[other], "seq", pairs).astype(F32)
        mine.append(summed.astype(BF16))
    back = [lax.all_to_all(rows, "exp", 0, 0, tiled=True) for rows in mine]
    expert_mix = pl.pallas_call(
        mix_kernel,
        out_shape=shape((local_tokens, features)),
        in_specs=[VMEM] * (2 + chunks),
        out_specs=VMEM,
        scratch_shapes=[pltpu.VMEM((EXPERTS * CAP, features), F32)],
        compiler_params=params(32),
        name="mix",
    )(expert_ids, route_weights, *back)
    return (attention, expert_mix)


def solution(mesh):
    return jax.shard_map(
        on_device,
        mesh=mesh,
        in_specs=(
            P(("seq", "exp"), None),
            P(),
            P(("seq", "exp"), None),
            P(("seq", "exp"), None),
            P(("seq", "exp"), None),
            P(("seq", "exp"), None),
            P(("seq", "exp"), None),
            P("exp", "seq", None),
            P("exp", "seq", None),
            P("exp", "seq", None),
        ),
        out_specs=(P(("seq", "exp"), None), P(("seq", "exp"), None)),
        check_vma=False,
    )
```

time: 207 us -> 165 us (0.80)
  matrix products: 42.1 us -> 0 us
  Pallas kernels: 0 us -> 40.6 us
  waiting for transfers between devices: 81.7 us -> 54.5 us
  blocking collectives: 0 us -> 21.6 us
  local copies, waits for them, and re-layouts: 25.1 us -> 7.8 us
  between operations: 14.3 us -> 0.81 us
  other arithmetic: 10.8 us -> 3.22 us
  starting transfers between devices: 31.6 us -> 35.5 us
    dot_general x11 -> x0, matrix products: 42.1 us -> none  [the longest x1 13.2 us: expert_block(): jnp.einsum('...ecf,efd->...ecd', hidden, down_proj, preferred_element_typ...]
    pallas_call x0 -> x7, Pallas kernels: none -> 40.6 us  [the longest x2 32.8 us: on_device(): pl.pallas_call(functools.partial(ffn_kernel, chunk * experts, seq_count),...]
    all_to_all x6 -> x5, waiting for transfers between devices: 65.5 us -> 31 us  [the longest x2 20.3 us: on_device(): back = [lax.all_to_all(rows, 'exp', 0, 0, tiled=True) for rows in mine]]
    ppermute x0 -> x7, waiting for transfers between devices: none -> 23.6 us  [the longest x2 12.7 us: on_device(): planes.append(lax.ppermute(recv[chunk], 'seq', pairs))]
    all_to_all x0 -> x1, blocking collectives: none -> 21.6 us  [on_device(): recv = [lax.all_to_all(rows, 'exp', 0, 0, tiled=True) for rows in send]]
    reduce_scatter x1 -> x0, waiting for transfers between devices: 15.4 us -> none  [on_device(): lax.psum_scatter(expert_block(gathered, gate_proj, up_proj, down_proj).as...]
    ppermute x0 -> x7, starting transfers between devices: none -> 14.1 us  [the longest x3 7.88 us: on_device(): parts.append(lax.ppermute(sums, everyone, pairs))]
    all_to_all x6 -> x5, starting transfers between devices: 31.2 us -> 21.4 us  [the longest x2 10.1 us: on_device(): back = [lax.all_to_all(rows, 'exp', 0, 0, tiled=True) for rows in mine]]
  transfers between devices with their start and end apart: 9 -> 12, of which waited for: 6 -> 6; matrix products, arithmetic and copies ran while one was open for 31% -> 2% of each run, Pallas kernels for 0% -> 23%
where the time goes in v1:
time: 165 us; the launch traced here: 164 us
  waiting for transfers between devices  54.5 us (33%)
  Pallas kernels  40.6 us (25%)
  starting transfers between devices  35.5 us (22%)
  blocking collectives  21.6 us (13%)
  local copies, waits for them, and re-layouts  7.8 us (5%)
  other arithmetic  3.22 us (2%)
    pallas_call x2, Pallas kernels, on_device(): pl.pallas_call(functools.partial(ffn_kernel, chunk * experts, seq_count),...  32.8 us
    all_to_all x1, blocking collectives, on_device(): recv = [lax.all_to_all(rows, 'exp', 0, 0, tiled=True) for rows in send]  21.6 us
    all_to_all x2, waiting for transfers between devices, on_device(): back = [lax.all_to_all(rows, 'exp', 0, 0, tiled=True) for rows in mine]  20.3 us
    ppermute x2, waiting for transfers between devices, on_device(): planes.append(lax.ppermute(recv[chunk], 'seq', pairs))  12.7 us
    all_to_all x1, waiting for transfers between devices, on_device(): recv = [lax.all_to_all(rows, 'exp', 0, 0, tiled=True) for rows in send]  10.7 us
    all_to_all x2, starting transfers between devices, on_device(): back = [lax.all_to_all(rows, 'exp', 0, 0, tiled=True) for rows in mine]  10.1 us
    ppermute x3, starting transfers between devices, on_device(): parts.append(lax.ppermute(sums, everyone, pairs))  7.88 us
    unnamed x24, local copies, waits for them, and re-layouts  7.08 us
  transfers between devices with their start and end apart: 12, of which 6 were waited for; matrix products, arithmetic and copies ran while one was open for 2% of the time, Pallas kernels for 23%

profile of v1, /device:TPU:0, one launch (start us, length us, event | category | flops | bytes accessed | tf_op | source)
XLA Modules:
  0.0 164.0 jit_solution(4950636710460106903)
XLA Ops:
  3.2 1.5 prep.1
  4.7 21.6 %all_to_all.30.refs_0_ = bf16[16,4,4096]{2,1,0:T(4,128)(2,1)S(1)} all-to-all(bf16[16,4,4096]{2,1,0:T(4,128)(2,1)S(1)} %get-tuple-element.11), channel_id=1, replica_groups=mesh['seq'=2,'exp'=16] {'exp'}, dimensions={0} | all-to-all | bytes 1048576 | tf_op jit(solution)/shard_map/all_to_all | solution.py:240
  26.3 4.1 %all-to-all-start.2 = ((bf16[16,4,4096]{2,1,0:T(4,128)(2,1)}), bf16[16,4,4096]{2,1,0:T(4,128)(2,1)S(1)}, u32[]{:S(2)}, u32[]{:S(2)}) async-start(bf16[16,4,4096]{2,1,0:T(4,128)(2,1)} %get-tuple-element.8), calls=%async_computation.2 | async-start | bytes 1048576 | tf_op jit(solution)/shard_map/all_to_all | solution.py:240
  34.2 10.7 %all-to-all-done.2.refs_0_ = bf16[16,4,4096]{2,1,0:T(4,128)(2,1)S(1)} async-done(((bf16[16,4,4096]{2,1,0:T(4,128)(2,1)}), bf16[16,4,4096]{2,1,0:T(4,128)(2,1)S(1)}, u32[]{:S(2)}, u32[]{:S(2)}) %all-to-all-start.2) | async-done | bytes 524320 | tf_op jit(solution)/shard_map/all_to_all | solution.py:240
  44.9 3.5 %all-to-all-start = ((bf16[8,3,64,256]{3,2,1,0:T(8,128)(2,1)}), bf16[8,3,64,256]{3,2,1,0:T(8,128)(2,1)S(1)}, u32[]{:S(2)}, u32[]{:S(2)}) async-start(bf16[8,3,64,256]{3,2,1,0:T(8,128)(2,1)} %pack.1), calls=%async_computation | async-start | bytes 1572864 | tf_op jit(solution)/shard_map/all_to_all | solution.py:238
  48.4 1.6 collective-permute-start.5
  50.5 12.7 %collective-permute-done.5.refs_1_ = bf16[16,4,4096]{2,1,0:T(4,128)(2,1)S(1)} collective-permute-done((bf16[16,4,4096]{2,1,0:T(4,128)(2,1)S(1)}, bf16[16,4,4096]{2,1,0:T(4,128)(2,1)S(1)}, u32[]{:S(2)}, u32[]{:S(2)}) %collective-permute-start.5) | collective-permute-done | bytes 524320 | tf_op jit(solution)/shard_map/ppermute | solution.py:279
  64.0 16.4 %experts.3 = (bf16[16,4,4096]{2,1,0:T(4,128)(2,1)}, bf16[16,4,4096]{2,1,0:T(4,128)(2,1)}) custom-call(bf16[16,4,4096]{2,1,0:T(4,128)(2,1)} %copy-done.6, bf16[16,4,4096]{2,1,0:T(4,128)(2,1)} %copy-done.8, bf16[4,704,4096]{2,1,0:T(8,128)(2,1)} %refs_2_.3, bf16[4,704,4096]{2,1,0:T(8,128)(2,1)} %refs_3_.3, bf16[4,704,4096]{2,1,0:T(8,128)(2,1)} %refs_4_.3), custom_call_target="tpu_custom_call" | custom-call | flops 2214592512 | bytes 34603008 | tf_op jit(solution)/shard_map/experts/pallas_call | solution.py:281
  80.5 1.6 collective-permute-start.6
  82.3 4.2 %collective-permute-start = (bf16[2,64,256]{2,1,0:T(8,128)(2,1)S(1)}, bf16[2,64,256]{2,1,0:T(8,128)(2,1)S(1)}, u32[]{:S(2)}, u32[]{:S(2)}) collective-permute-start(bf16[2,64,256]{2,1,0:T(8,128)(2,1)S(1)} %sums.1), channel_id=1, source_target_pairs={{0,8},{1,9},{2,10},{3,11},{4,12},{5,13},{6,14},{7,15},{8,16},{9,17... | collective-permute-start | bytes 196616 | tf_op jit(solution)/shard_map/ppermute | solution.py:260
  86.5 2.4 %collective-permute-start.1 = (bf16[2,64,256]{2,1,0:T(8,128)(2,1)S(1)}, bf16[2,64,256]{2,1,0:T(8,128)(2,1)S(1)}, u32[]{:S(2)}, u32[]{:S(2)}) collective-permute-start(bf16[2,64,256]{2,1,0:T(8,128)(2,1)S(1)} %sums.1), channel_id=1, source_target_pairs={{0,16},{1,17},{2,18},{3,19},{4,20},{5,21},{6,22},{7,23},{8,24},{9,... | collective-permute-start | bytes 196616 | tf_op jit(solution)/shard_map/ppermute | solution.py:260
  88.9 1.3 collective-permute-start.2
  90.2 5.2 %collective-permute-done.1.refs_1_ = bf16[2,64,256]{2,1,0:T(8,128)(2,1)S(1)} collective-permute-done((bf16[2,64,256]{2,1,0:T(8,128)(2,1)S(1)}, bf16[2,64,256]{2,1,0:T(8,128)(2,1)S(1)}, u32[]{:S(2)}, u32[]{:S(2)}) %collective-permute-start.1) | collective-permute-done | bytes 65568 | tf_op jit(solution)/shard_map/ppermute | solution.py:260
  95.4 3.4 %attend.1 = bf16[512,256]{1,0:T(8,128)(2,1)} custom-call(s32[1]{0:T(128)} %bitcast.seg_ref, bf16[8,3,64,256]{3,2,1,0:T(8,128)(2,1)S(1)} %all-to-all-done.recv_ref, bf16[2,64,256]{2,1,0:T(8,128)(2,1)S(1)} %collective-permute-done.refs_0_, bf16[2,64,256]{2,1,0:T(8,128)(2,1)S(1)} %collective-permute-done.1.refs_1_, ...), custom_call_target="tpu_custom_call" | custom-call | tf_op jit(solution)/shard_map/attend/pallas_call | solution.py:261
  98.8 3.6 %all-to-all-start.1 = ((bf16[8,64,256]{2,1,0:T(8,128)(2,1)}), bf16[8,64,256]{2,1,0:T(8,128)(2,1)S(1)}, u32[]{:S(2)}, u32[]{:S(2)}) async-start(bf16[8,64,256]{2,1,0:T(8,128)(2,1)} %bitcast.1), calls=%async_computation.1 | async-start | bytes 524288 | tf_op jit(solution)/shard_map/all_to_all | solution.py:269
  103.3 16.4 %experts.2 = (bf16[16,4,4096]{2,1,0:T(4,128)(2,1)}, bf16[16,4,4096]{2,1,0:T(4,128)(2,1)}) custom-call(bf16[16,4,4096]{2,1,0:T(4,128)(2,1)} %copy-done.5, bf16[16,4,4096]{2,1,0:T(4,128)(2,1)} %copy-done.7, bf16[4,704,4096]{2,1,0:T(8,128)(2,1)} %refs_2_.3, bf16[4,704,4096]{2,1,0:T(8,128)(2,1)} %refs_3_.3, bf16[4,704,4096]{2,1,0:T(8,128)(2,1)} %refs_4_.3), custom_call_target="tpu_custom_call" | custom-call | flops 2214592512 | bytes 34603008 | tf_op jit(solution)/shard_map/experts/pallas_call | solution.py:281
  119.7 2.5 %collective-permute-start.4 = (bf16[16,4,4096]{2,1,0:T(4,128)(2,1)}, bf16[16,4,4096]{2,1,0:T(4,128)(2,1)S(1)}, u32[]{:S(2)}, u32[]{:S(2)}) collective-permute-start(bf16[16,4,4096]{2,1,0:T(4,128)(2,1)} %get-tuple-element.10), channel_id=1, source_target_pairs={{0,16},{16,0},{1,17},{17,1},{2,18},{18,2},{3,19},{19,3},{4,20},{20... | collective-permute-start | bytes 1572872 | tf_op jit(solution)/shard_map/ppermute | solution.py:303
  123.4 6.0 %all-to-all-start.5 = ((bf16[16,4,4096]{2,1,0:T(4,128)(2,1)}), bf16[16,4,4096]{2,1,0:T(4,128)(2,1)S(1)}, u32[]{:S(2)}, u32[]{:S(2)}) async-start(bf16[16,4,4096]{2,1,0:T(4,128)(2,1)} %add_convert_fusion), calls=%async_computation.5 | async-start | bytes 1048576 | tf_op jit(solution)/shard_map/all_to_all | solution.py:305
  129.4 5.7 %collective-permute-done.4 = bf16[16,4,4096]{2,1,0:T(4,128)(2,1)S(1)} collective-permute-done((bf16[16,4,4096]{2,1,0:T(4,128)(2,1)}, bf16[16,4,4096]{2,1,0:T(4,128)(2,1)S(1)}, u32[]{:S(2)}, u32[]{:S(2)}) %collective-permute-start.4) | collective-permute-done | bytes 524320 | tf_op jit(solution)/shard_map/ppermute | solution.py:303
  135.1 2.1 %add_convert_fusion.1 = bf16[16,4,4096]{2,1,0:T(4,128)(2,1)} fusion(bf16[16,4,4096]{2,1,0:T(4,128)(2,1)S(1)} %collective-permute-done.4, bf16[16,4,4096]{2,1,0:T(4,128)(2,1)} %get-tuple-element.9), kind=kLoop, calls=%fused_computation.1 | loop fusion | flops 1048576 | bytes 1572864 | tf_op jit(solution)/shard_map/convert_element_type | solution.py:304
  137.2 6.7 %all-to-all-done.5.refs_1_ = bf16[16,4,4096]{2,1,0:T(4,128)(2,1)S(1)} async-done(((bf16[16,4,4096]{2,1,0:T(4,128)(2,1)}), bf16[16,4,4096]{2,1,0:T(4,128)(2,1)S(1)}, u32[]{:S(2)}, u32[]{:S(2)}) %all-to-all-start.5) | async-done | bytes 524320 | tf_op jit(solution)/shard_map/all_to_all | solution.py:305
  143.8 4.1 %all-to-all-start.3 = ((bf16[16,4,4096]{2,1,0:T(4,128)(2,1)}), bf16[16,4,4096]{2,1,0:T(4,128)(2,1)S(1)}, u32[]{:S(2)}, u32[]{:S(2)}) async-start(bf16[16,4,4096]{2,1,0:T(4,128)(2,1)} %add_convert_fusion.1), calls=%async_computation.3 | async-start | bytes 1048576 | tf_op jit(solution)/shard_map/all_to_all | solution.py:305
  148.8 13.6 %all-to-all-done.3.refs_0_ = bf16[16,4,4096]{2,1,0:T(4,128)(2,1)S(1)} async-done(((bf16[16,4,4096]{2,1,0:T(4,128)(2,1)}), bf16[16,4,4096]{2,1,0:T(4,128)(2,1)S(1)}, u32[]{:S(2)}, u32[]{:S(2)}) %all-to-all-start.3) | async-done | bytes 524320 | tf_op jit(solution)/shard_map/all_to_all | solution.py:305
  162.4 1.6 mix.1
  (35 shorter events, 10.6 us)
Async XLA Ops:
  1.4 1.0 copy-start
  2.4 0.7 copy-start.4
  26.3 36.9 %copy-start.6 = (bf16[16,4,4096]{2,1,0:T(4,128)(2,1)}, bf16[16,4,4096]{2,1,0:T(4,128)(2,1)S(1)}, u32[]{:S(2)}) copy-start(bf16[16,4,4096]{2,1,0:T(4,128)(2,1)S(1)} %all_to_all.30.refs_0_) | copy-start | bytes 1572868
  26.3 18.6 %all-to-all-start.2 = ((bf16[16,4,4096]{2,1,0:T(4,128)(2,1)}), bf16[16,4,4096]{2,1,0:T(4,128)(2,1)S(1)}, u32[]{:S(2)}, u32[]{:S(2)}) async-start(bf16[16,4,4096]{2,1,0:T(4,128)(2,1)} %get-tuple-element.8), calls=%async_computation.2 | async-start | bytes 1048576 | tf_op jit(solution)/shard_map/all_to_all | solution.py:240
  30.4 1.0 copy-start.1
  31.4 0.9 copy-start.2
  32.3 0.9 copy-start.3
  44.9 35.6 %copy-start.5 = (bf16[16,4,4096]{2,1,0:T(4,128)(2,1)}, bf16[16,4,4096]{2,1,0:T(4,128)(2,1)S(1)}, u32[]{:S(2)}) copy-start(bf16[16,4,4096]{2,1,0:T(4,128)(2,1)S(1)} %all-to-all-done.2.refs_0_) | copy-start | bytes 1572868
  44.9 37.2 %all-to-all-start = ((bf16[8,3,64,256]{3,2,1,0:T(8,128)(2,1)}), bf16[8,3,64,256]{3,2,1,0:T(8,128)(2,1)S(1)}, u32[]{:S(2)}, u32[]{:S(2)}) async-start(bf16[8,3,64,256]{3,2,1,0:T(8,128)(2,1)} %pack.1), calls=%async_computation | async-start | bytes 1572864 | tf_op jit(solution)/shard_map/all_to_all | solution.py:238
  48.4 14.8 %collective-permute-start.5 = (bf16[16,4,4096]{2,1,0:T(4,128)(2,1)S(1)}, bf16[16,4,4096]{2,1,0:T(4,128)(2,1)S(1)}, u32[]{:S(2)}, u32[]{:S(2)}) collective-permute-start(bf16[16,4,4096]{2,1,0:T(4,128)(2,1)S(1)} %all_to_all.30.refs_0_), channel_id=1, source_target_pairs={{0,16},{16,0},{1,17},{17,1},{2,18},{18,2},{3,19},{19,3},{4,20},{20... | collective-permute-start | bytes 1572872 | tf_op jit(solution)/shard_map/ppermute | solution.py:279
  50.0 52.5 %collective-permute-start.3 = (bf16[16,4,4096]{2,1,0:T(4,128)(2,1)S(1)}, bf16[16,4,4096]{2,1,0:T(4,128)(2,1)S(1)}, u32[]{:S(2)}, u32[]{:S(2)}) collective-permute-start(bf16[16,4,4096]{2,1,0:T(4,128)(2,1)S(1)} %all-to-all-done.2.refs_0_), channel_id=1, source_target_pairs={{0,16},{16,0},{1,17},{17,1},{2,18},{18,2},{3,19},{19,3},{4,20},{20... | collective-permute-start | bytes 1572872 | tf_op jit(solution)/shard_map/ppermute | solution.py:279
  63.2 0.8 copy-start.8
  80.5 41.8 %collective-permute-start.6 = (bf16[16,4,4096]{2,1,0:T(4,128)(2,1)}, bf16[16,4,4096]{2,1,0:T(4,128)(2,1)S(1)}, u32[]{:S(2)}, u32[]{:S(2)}) collective-permute-start(bf16[16,4,4096]{2,1,0:T(4,128)(2,1)} %get-tuple-element.13), channel_id=1, source_target_pairs={{0,16},{16,0},{1,17},{17,1},{2,18},{18,2},{3,19},{19,3},{4,20},{20... | collective-permute-start | bytes 1572872 | tf_op jit(solution)/shard_map/ppermute | solution.py:303
  82.3 7.9 %collective-permute-start = (bf16[2,64,256]{2,1,0:T(8,128)(2,1)S(1)}, bf16[2,64,256]{2,1,0:T(8,128)(2,1)S(1)}, u32[]{:S(2)}, u32[]{:S(2)}) collective-permute-start(bf16[2,64,256]{2,1,0:T(8,128)(2,1)S(1)} %sums.1), channel_id=1, source_target_pairs={{0,8},{1,9},{2,10},{3,11},{4,12},{5,13},{6,14},{7,15},{8,16},{9,17... | collective-permute-start | bytes 196616 | tf_op jit(solution)/shard_map/ppermute | solution.py:260
  86.5 8.9 %collective-permute-start.1 = (bf16[2,64,256]{2,1,0:T(8,128)(2,1)S(1)}, bf16[2,64,256]{2,1,0:T(8,128)(2,1)S(1)}, u32[]{:S(2)}, u32[]{:S(2)}) collective-permute-start(bf16[2,64,256]{2,1,0:T(8,128)(2,1)S(1)} %sums.1), channel_id=1, source_target_pairs={{0,16},{1,17},{2,18},{3,19},{4,20},{5,21},{6,22},{7,23},{8,24},{9,... | collective-permute-start | bytes 196616 | tf_op jit(solution)/shard_map/ppermute | solution.py:260
  88.9 6.5 %collective-permute-start.2 = (bf16[2,64,256]{2,1,0:T(8,128)(2,1)S(1)}, bf16[2,64,256]{2,1,0:T(8,128)(2,1)S(1)}, u32[]{:S(2)}, u32[]{:S(2)}) collective-permute-start(bf16[2,64,256]{2,1,0:T(8,128)(2,1)S(1)} %sums.1), channel_id=1, source_target_pairs={{0,24},{1,25},{2,26},{3,27},{4,28},{5,29},{6,30},{7,31}} | collective-permute-start | bytes 196616 | tf_op jit(solution)/shard_map/ppermute | solution.py:260
  98.8 24.6 %all-to-all-start.1 = ((bf16[8,64,256]{2,1,0:T(8,128)(2,1)}), bf16[8,64,256]{2,1,0:T(8,128)(2,1)S(1)}, u32[]{:S(2)}, u32[]{:S(2)}) async-start(bf16[8,64,256]{2,1,0:T(8,128)(2,1)} %bitcast.1), calls=%async_computation.1 | async-start | bytes 524288 | tf_op jit(solution)/shard_map/all_to_all | solution.py:269
  102.5 19.8 %copy-start.9 = (bf16[16,4,4096]{2,1,0:T(4,128)(2,1)S(1)}, bf16[16,4,4096]{2,1,0:T(4,128)(2,1)}, u32[]{:S(2)}) copy-start(bf16[16,4,4096]{2,1,0:T(4,128)(2,1)} %get-tuple-element.12) | copy-start | bytes 1572868
  102.5 45.5 %copy-start.10 = (f32[64,2]{0,1:T(2,128)S(1)}, f32[64,2]{0,1:T(2,128)}, u32[]{:S(2)}) copy-start(f32[64,2]{0,1:T(2,128)} %param.16) | copy-start | bytes 1540
  102.5 0.8 copy-start.7
  119.7 15.3 %collective-permute-start.4 = (bf16[16,4,4096]{2,1,0:T(4,128)(2,1)}, bf16[16,4,4096]{2,1,0:T(4,128)(2,1)S(1)}, u32[]{:S(2)}, u32[]{:S(2)}) collective-permute-start(bf16[16,4,4096]{2,1,0:T(4,128)(2,1)} %get-tuple-element.10), channel_id=1, source_target_pairs={{0,16},{16,0},{1,17},{17,1},{2,18},{18,2},{3,19},{19,3},{4,20},{20... | collective-permute-start | bytes 1572872 | tf_op jit(solution)/shard_map/ppermute | solution.py:303
  123.4 20.5 %all-to-all-start.5 = ((bf16[16,4,4096]{2,1,0:T(4,128)(2,1)}), bf16[16,4,4096]{2,1,0:T(4,128)(2,1)S(1)}, u32[]{:S(2)}, u32[]{:S(2)}) async-start(bf16[16,4,4096]{2,1,0:T(4,128)(2,1)} %add_convert_fusion), calls=%async_computation.5 | async-start | bytes 1048576 | tf_op jit(solution)/shard_map/all_to_all | solution.py:305
  143.8 18.6 %all-to-all-start.3 = ((bf16[16,4,4096]{2,1,0:T(4,128)(2,1)}), bf16[16,4,4096]{2,1,0:T(4,128)(2,1)S(1)}, u32[]{:S(2)}, u32[]{:S(2)}) async-start(bf16[16,4,4096]{2,1,0:T(4,128)(2,1)} %add_convert_fusion.1), calls=%async_computation.3 | async-start | bytes 1048576 | tf_op jit(solution)/shard_map/all_to_all | solution.py:305
